TPU v7x, 512 devices: a whole 4x8x8 slice. The times are simulated.
512 devices in a mesh: section: 16 (over y_lo, z), expert: 32 (over x, y_hi, core).
Axes of the slice: x: 4, y: 8 (y_hi: 4, y_lo: 2; y = y_hi * 2 + y_lo), z: 8, core: 2. Of those that a mesh axis runs over, the one named last changes fastest.
Arguments:
- act_fwd: bfloat16 [16, 256, 3584], P('section', 'expert'), may hold values from -6 to 6
- route_fwd: int32 [16, 256, 2], P('section', 'expert'), may hold values from 0 to 3, as said below
- slot_fwd: int32 [16, 256, 2], P('section', 'expert'), may hold values from 0 to 7, as said below
- weight_fwd: float32 [16, 256, 2], P('section', 'expert'), may hold values from 0.1 to 1
- grad_bwd: bfloat16 [16, 256, 3584], P('section', 'expert'), may hold values from -6 to 6
- route_bwd: int32 [16, 256, 2], P('section', 'expert'), may hold values from 0 to 3, as said below
- slot_bwd: int32 [16, 256, 2], P('section', 'expert'), may hold values from 0 to 7, as said below
- weight_bwd: float32 [16, 256, 2], P('section', 'expert'), may hold values from 0.1 to 1
- saved_gate: bfloat16 [16, 32, 8, 4096], P('section', None, None, 'expert'), may hold values from -6 to 6
- saved_up: bfloat16 [16, 32, 8, 4096], P('section', None, None, 'expert'), may hold values from -6 to 6
- w_gate: bfloat16 [16, 3584, 4096], P('section', None, 'expert'), may hold values from -0.09375 to 0.09375
- w_up: bfloat16 [16, 3584, 4096], P('section', None, 'expert'), may hold values from -0.09375 to 0.09375
- w_down: bfloat16 [16, 4096, 3584], P('section', 'expert'), may hold values from -0.1875 to 0.1875
Outputs:
- fwd_next: bfloat16 [16, 256, 3584], P('section', 'expert')
- bwd_prev: bfloat16 [16, 256, 3584], P('section', 'expert')
Inputs may be any that keep to these rules, and one draw needn't show every extreme that they name: `route_fwd`: each token names 2 different experts. Within the 8 tokens of one block, no expert is named more than 8 times, and one expert is named exactly 8 times. `slot_fwd`: within one block, the tokens naming one expert hold distinct slots 0 to their count - 1. `route_bwd`: as for route_fwd. `slot_bwd`: as for slot_fwd, with route_bwd.
All inputs are finite; a program needn't handle non-finite values.
Results may differ from a plain program's by a relative error of at most 0.005.
Values may be sent and summed in bfloat16 or wider, within the bound.
A program may use at most 64 MiB of HBM per device.

v0:
```python
import jax
import jax.numpy as jnp
from jax import lax
from jax.sharding import PartitionSpec as P

EXP_WIN = 4


def passed_along(array, axis, by):
    peers = lax.axis_size(axis)
    return lax.ppermute(array, axis, [(i, (i + by) % peers) for i in range(peers)])


def outgoing(tokens, route, slot, experts, capacity, group):
    count = tokens.shape[0]
    matched = (
        route[:, :, None, None] == jnp.arange(experts, dtype=jnp.int32)[None, None, :, None]
    ) & (slot[:, :, None, None] == jnp.arange(capacity, dtype=jnp.int32)[None, None, None, :])
    taken = jnp.any(matched, axis=1)
    position = jnp.sum(
        taken.astype(jnp.int32) * jnp.arange(count, dtype=jnp.int32)[:, None, None], axis=0
    )
    filled = jnp.any(taken, axis=0)
    picked = jnp.where(filled[:, :, None], tokens[position], jnp.zeros((), tokens.dtype))
    return jnp.repeat(picked, group, axis=0)


def forward_local(block, gate_cols, up_cols, down_rows):
    flat = block.reshape(-1, block.shape[-1])
    gate_val = jnp.dot(flat, gate_cols, preferred_element_type=jnp.float32)
    up_val = jnp.dot(flat, up_cols, preferred_element_type=jnp.float32)
    hidden = (jax.nn.silu(gate_val) * up_val).astype(jnp.bfloat16)
    result = jnp.dot(hidden, down_rows, preferred_element_type=jnp.float32).astype(jnp.bfloat16)
    return result.reshape(block.shape)


def backward_local(block, gate_saved, up_saved, gate_cols, up_cols, down_rows):
    flat = block.reshape(-1, block.shape[-1])
    grad_hidden = jnp.dot(flat, down_rows.T, preferred_element_type=jnp.float32)
    gate_val = gate_saved.reshape(grad_hidden.shape).astype(jnp.float32)
    up_val = up_saved.reshape(grad_hidden.shape).astype(jnp.float32)
    sigma = jax.nn.sigmoid(gate_val)
    slope = sigma * (1.0 + gate_val * (1.0 - sigma))
    grad_gate = (grad_hidden * up_val * slope).astype(jnp.bfloat16)
    grad_up = (grad_hidden * gate_val * sigma).astype(jnp.bfloat16)
    result = jnp.dot(grad_gate, gate_cols.T, preferred_element_type=jnp.float32)
    result = result + jnp.dot(grad_up, up_cols.T, preferred_element_type=jnp.float32)
    return result.astype(jnp.bfloat16).reshape(block.shape)


def send_back(partial_value):
    return lax.all_to_all(partial_value, "expert", split_axis=0, concat_axis=0, tiled=True)


def combine_local(base, back, route, slot, weight, experts):
    owners, capacity, width = back.shape
    group = owners // experts
    total = jnp.sum(back.reshape(experts, group, capacity, width).astype(jnp.float32), axis=1)
    total = total.reshape(experts * capacity, width)
    gathered = total[route * capacity + slot]
    return (base.astype(jnp.float32) + jnp.sum(weight[:, :, None] * gathered, axis=1)).astype(
        jnp.bfloat16
    )


def local(
    act_fwd,
    route_fwd,
    slot_fwd,
    weight_fwd,
    grad_bwd,
    route_bwd,
    slot_bwd,
    weight_bwd,
    saved_gate,
    saved_up,
    w_gate,
    w_up,
    w_down,
):
    tokens = act_fwd[0]
    grads = grad_bwd[0]
    capacity = saved_gate.shape[2]
    experts = EXP_WIN
    group = lax.axis_size("expert") // experts
    gate_cols = w_gate[0]
    up_cols = w_up[0]
    down_rows = w_down[0]
    send_fwd = outgoing(tokens, route_fwd[0], slot_fwd[0], experts, capacity, group)
    part_fwd = forward_local(
        lax.all_to_all(send_fwd, "expert", split_axis=0, concat_axis=0, tiled=True),
        gate_cols,
        up_cols,
        down_rows,
    )
    send_bwd = outgoing(grads, route_bwd[0], slot_bwd[0], experts, capacity, group)
    rows_bwd = lax.all_to_all(send_bwd, "expert", split_axis=0, concat_axis=0, tiled=True)
    back_fwd = send_back(part_fwd)
    part_bwd = backward_local(rows_bwd, saved_gate[0], saved_up[0], gate_cols, up_cols, down_rows)
    back_bwd = send_back(part_bwd)
    layer_out = combine_local(tokens, back_fwd, route_fwd[0], slot_fwd[0], weight_fwd[0], experts)
    input_grad = combine_local(grads, back_bwd, route_bwd[0], slot_bwd[0], weight_bwd[0], experts)
    fwd_next = passed_along(layer_out[None], "section", 1)
    bwd_prev = passed_along(input_grad[None], "section", -1)
    return (fwd_next, bwd_prev)


def solution(mesh):
    in_specs = (
        P("section", "expert", None),
        P("section", "expert", None),
        P("section", "expert", None),
        P("section", "expert", None),
        P("section", "expert", None),
        P("section", "expert", None),
        P("section", "expert", None),
        P("section", "expert", None),
        P("section", None, None, "expert"),
        P("section", None, None, "expert"),
        P("section", None, "expert"),
        P("section", None, "expert"),
        P("section", "expert", None),
    )
    out_specs = (P("section", "expert", None), P("section", "expert", None))
    return jax.shard_map(local, mesh=mesh, in_specs=in_specs, out_specs=out_specs, check_vma=False)
```

profile of v0, /device:TPU:8, one launch (start us, length us, event | category | flops | bytes accessed | tf_op | source)
XLA Modules:
  0.0 232.3 jit_solution(7121170864156542958)
XLA Ops:
  0.6 0.8 iota_compare_fusion
  1.5 0.7 iota_compare_fusion.2
  2.2 0.1 and_reduce_fusion.1
  2.3 0.1 reshape.196
  2.4 1.7 gather_fusion.2
  4.1 0.1 bitcast_select_fusion
  4.2 1.4 broadcast_in_dim.42
  5.6 9.2 %all-to-all-start.2 = ((bf16[32,8,3584]{2,1,0:T(8,128)(2,1)}), bf16[32,8,3584]{2,1,0:T(8,128)(2,1)S(1)}, u32[]{:S(2)}, u32[]{:S(2)}) async-start(bf16[32,8,3584]{2,1,0:T(8,128)(2,1)} %bitcast.100), calls=%async_computation.2 | async-start | bytes 3670016 | tf_op jit(solution)/shard_map/all_to_all | solution.py:97
  14.8 0.1 iota_compare_fusion.1
  14.9 0.1 and_reduce_fusion.3
  15.0 0.1 reshape.180
  15.1 0.7 gather_fusion
  15.8 0.1 bitcast_select_fusion.1
  15.9 38.4 %all-to-all-done.2 = bf16[32,8,3584]{2,1,0:T(8,128)(2,1)S(1)} async-done(((bf16[32,8,3584]{2,1,0:T(8,128)(2,1)}), bf16[32,8,3584]{2,1,0:T(8,128)(2,1)S(1)}, u32[]{:S(2)}, u32[]{:S(2)}) %all-to-all-start.2) | async-done | bytes 1835040 | tf_op jit(solution)/shard_map/all_to_all | solution.py:97
  54.3 1.5 broadcast_in_dim.40
  55.7 0.3 copy-done.3
  56.1 10.6 %all-to-all-start = ((bf16[32,8,3584]{2,1,0:T(8,128)(2,1)}), bf16[32,8,3584]{2,1,0:T(8,128)(2,1)S(1)}, u32[]{:S(2)}, u32[]{:S(2)}) async-start(bf16[32,8,3584]{2,1,0:T(8,128)(2,1)} %bitcast.101), calls=%async_computation | async-start | bytes 3670016 | tf_op jit(solution)/shard_map/all_to_all | solution.py:91
  66.7 2.4 %fusion.3 = f32[256,128]{1,0:T(8,128)S(1)} fusion(bf16[32,8,3584]{2,1,0:T(8,128)(2,1)} %copy-done.3, bf16[1,128,3584]{2,1,0:T(8,128)(2,1)} %param.25), kind=kOutput, calls=%fused_computation.11 | convolution fusion | flops 234881024 | bytes 2883584 | tf_op jit(solution)/shard_map/dot_general | solution.py:39
  69.2 0.7 fusion.22
  69.9 1.9 fusion.2
  71.8 32.2 %all-to-all-done = bf16[32,8,3584]{2,1,0:T(8,128)(2,1)S(1)} async-done(((bf16[32,8,3584]{2,1,0:T(8,128)(2,1)}), bf16[32,8,3584]{2,1,0:T(8,128)(2,1)S(1)}, u32[]{:S(2)}, u32[]{:S(2)}) %all-to-all-start) | async-done | bytes 1835040 | tf_op jit(solution)/shard_map/all_to_all | solution.py:91
  104.0 13.3 %all-to-all-start.3 = ((bf16[32,8,3584]{2,1,0:T(8,128)(2,1)}), bf16[32,8,3584]{2,1,0:T(8,128)(2,1)}, u32[]{:S(2)}, u32[]{:S(2)}) async-start(bf16[32,8,3584]{2,1,0:T(8,128)(2,1)} %fusion.2), calls=%async_computation.3 | async-start | bytes 3670016 | tf_op jit(solution)/shard_map/all_to_all | solution.py:52
  117.4 1.8 fusion.7
  119.2 3.6 %fusion.1 = bf16[32,8,3584]{2,1,0:T(8,128)(2,1)} fusion(bf16[32,8,3584]{2,1,0:T(8,128)(2,1)S(1)} %all-to-all-done, bf16[1,128,3584]{2,1,0:T(8,128)(2,1)} %param.25, bf16[1,3584,128]{2,1,0:T(8,128)(2,1)S(1)} %copy-done, f32[256,128]{1,0:T(8,128)S(1)} %fusion.7), kind=kOutput, calls=%fused_computation.7 | convolution fusion | flops 470876160 | bytes 5636096 | tf_op jit(solution)/shard_map/dot_general | solution.py:33
  122.8 33.0 %all-to-all-done.3 = bf16[32,8,3584]{2,1,0:T(8,128)(2,1)} async-done(((bf16[32,8,3584]{2,1,0:T(8,128)(2,1)}), bf16[32,8,3584]{2,1,0:T(8,128)(2,1)}, u32[]{:S(2)}, u32[]{:S(2)}) %all-to-all-start.3) | async-done | bytes 1835040 | tf_op jit(solution)/shard_map/all_to_all | solution.py:52
  155.8 12.7 %all-to-all-start.1 = ((bf16[32,8,3584]{2,1,0:T(8,128)(2,1)}), bf16[32,8,3584]{2,1,0:T(8,128)(2,1)S(1)}, u32[]{:S(2)}, u32[]{:S(2)}) async-start(bf16[32,8,3584]{2,1,0:T(8,128)(2,1)} %fusion.1), calls=%async_computation.1 | async-start | bytes 3670016 | tf_op jit(solution)/shard_map/all_to_all | solution.py:52
  168.6 0.1 copy.34
  168.7 0.1 reshape.204
  168.7 0.7 copy.33
  169.4 0.1 copy.32
  169.5 0.1 reshape.188
  169.6 0.7 copy.31
  170.3 0.6 pad_clamp_fusion
  170.9 0.6 pad_clamp_fusion.2
  171.5 1.8 convert_reduce_fusion
  173.3 0.9 gather_fusion.3
  174.2 0.1 reshape.203
  174.3 1.0 multiply_reduce_fusion
  175.4 12.3 %collective-permute-start.1 = (bf16[1,8,3584]{2,1,0:T(8,128)(2,1)S(1)}, bf16[1,8,3584]{2,1,0:T(8,128)(2,1)S(1)}, u32[]{:S(2)}, u32[]{:S(2)}) collective-permute-start(bf16[1,8,3584]{2,1,0:T(8,128)(2,1)S(1)} %fusion.39), channel_id=1, source_target_pairs={{0,480},{32,0},{64,32},{96,64},{128,96},{160,128},{192,160},{224,1... | collective-permute-start | bytes 172040 | tf_op jit(solution)/shard_map/ppermute | solution.py:11
  187.7 20.5 %all-to-all-done.1 = bf16[32,8,3584]{2,1,0:T(8,128)(2,1)S(1)} async-done(((bf16[32,8,3584]{2,1,0:T(8,128)(2,1)}), bf16[32,8,3584]{2,1,0:T(8,128)(2,1)S(1)}, u32[]{:S(2)}, u32[]{:S(2)}) %all-to-all-start.1) | async-done | bytes 1835040 | tf_op jit(solution)/shard_map/all_to_all | solution.py:52
  208.2 0.3 convert_reduce_fusion.1
  208.5 0.6 gather_fusion.1
  209.1 0.1 reshape.187
  209.2 0.4 multiply_reduce_fusion.1
  209.6 4.3 %collective-permute-start = (bf16[1,8,3584]{2,1,0:T(8,128)(2,1)S(1)}, bf16[1,8,3584]{2,1,0:T(8,128)(2,1)S(1)}, u32[]{:S(2)}, u32[]{:S(2)}) collective-permute-start(bf16[1,8,3584]{2,1,0:T(8,128)(2,1)S(1)} %fusion.40), channel_id=1, source_target_pairs={{0,32},{32,64},{64,96},{96,128},{128,160},{160,192},{192,224},{224... | collective-permute-start | bytes 172040 | tf_op jit(solution)/shard_map/ppermute | solution.py:11
  213.9 17.1 %collective-permute-done = bf16[1,8,3584]{2,1,0:T(8,128)(2,1)S(1)} collective-permute-done((bf16[1,8,3584]{2,1,0:T(8,128)(2,1)S(1)}, bf16[1,8,3584]{2,1,0:T(8,128)(2,1)S(1)}, u32[]{:S(2)}, u32[]{:S(2)}) %collective-permute-start) | collective-permute-done | bytes 57376 | tf_op jit(solution)/shard_map/ppermute | solution.py:11
  231.0 0.6 copy.37
  231.7 0.6 copy.38
  (41 shorter events, 0.2 us)
Async XLA Ops:
  0.6 69.2 %copy-start = (bf16[1,3584,128]{2,1,0:T(8,128)(2,1)S(1)}, bf16[1,3584,128]{2,1,0:T(8,128)(2,1)}, u32[]{:S(2)}) copy-start(bf16[1,3584,128]{2,1,0:T(8,128)(2,1)} %param.24) | copy-start | bytes 2752516
  5.6 9.2 %copy-start.12 = (s32[1,8,2]{1,2,0:T(2,128)S(1)}, s32[1,8,2]{1,2,0:T(2,128)}, u32[]{:S(2)}) copy-start(s32[1,8,2]{1,2,0:T(2,128)} %param.14) | copy-start | bytes 196
  5.6 9.2 %copy-start.10 = (s32[1,8,2]{1,2,0:T(2,128)S(1)}, s32[1,8,2]{1,2,0:T(2,128)}, u32[]{:S(2)}) copy-start(s32[1,8,2]{1,2,0:T(2,128)} %param.15) | copy-start | bytes 196
  5.6 9.5 %copy-start.2 = (bf16[1,8,3584]{2,1,0:T(8,128)(2,1)S(1)}, bf16[1,8,3584]{2,1,0:T(8,128)(2,1)}, u32[]{:S(2)}) copy-start(bf16[1,8,3584]{2,1,0:T(8,128)(2,1)} %param.13) | copy-start | bytes 172036
  5.6 48.7 %all-to-all-start.2 = ((bf16[32,8,3584]{2,1,0:T(8,128)(2,1)}), bf16[32,8,3584]{2,1,0:T(8,128)(2,1)S(1)}, u32[]{:S(2)}, u32[]{:S(2)}) async-start(bf16[32,8,3584]{2,1,0:T(8,128)(2,1)} %bitcast.100), calls=%async_computation.2 | async-start | bytes 3670016 | tf_op jit(solution)/shard_map/all_to_all | solution.py:97
  54.3 1.8 copy-start.3
  56.1 47.9 %all-to-all-start = ((bf16[32,8,3584]{2,1,0:T(8,128)(2,1)}), bf16[32,8,3584]{2,1,0:T(8,128)(2,1)S(1)}, u32[]{:S(2)}, u32[]{:S(2)}) async-start(bf16[32,8,3584]{2,1,0:T(8,128)(2,1)} %bitcast.101), calls=%async_computation | async-start | bytes 3670016 | tf_op jit(solution)/shard_map/all_to_all | solution.py:91
  66.7 2.5 %copy-start.4 = (bf16[1,3584,128]{2,1,0:T(8,128)(2,1)S(1)}, bf16[1,3584,128]{2,1,0:T(8,128)(2,1)}, u32[]{:S(2)}) copy-start(bf16[1,3584,128]{2,1,0:T(8,128)(2,1)} %param.23) | copy-start | bytes 2752516
  66.7 2.5 %copy-start.5 = (bf16[1,32,8,128]{3,2,1,0:T(8,128)(2,1)S(1)}, bf16[1,32,8,128]{3,2,1,0:T(8,128)(2,1)}, u32[]{:S(2)}) copy-start(bf16[1,32,8,128]{3,2,1,0:T(8,128)(2,1)} %param.21) | copy-start | bytes 196612
  66.7 2.5 %copy-start.6 = (bf16[1,32,8,128]{3,2,1,0:T(8,128)(2,1)S(1)}, bf16[1,32,8,128]{3,2,1,0:T(8,128)(2,1)}, u32[]{:S(2)}) copy-start(bf16[1,32,8,128]{3,2,1,0:T(8,128)(2,1)} %param.22) | copy-start | bytes 196612
  104.0 51.8 %all-to-all-start.3 = ((bf16[32,8,3584]{2,1,0:T(8,128)(2,1)}), bf16[32,8,3584]{2,1,0:T(8,128)(2,1)}, u32[]{:S(2)}, u32[]{:S(2)}) async-start(bf16[32,8,3584]{2,1,0:T(8,128)(2,1)} %fusion.2), calls=%async_computation.3 | async-start | bytes 3670016 | tf_op jit(solution)/shard_map/all_to_all | solution.py:52
  122.8 45.7 %copy-start.9 = (s32[1,8,2]{1,2,0:T(2,128)S(1)}, s32[1,8,2]{1,2,0:T(2,128)}, u32[]{:S(2)}) copy-start(s32[1,8,2]{1,2,0:T(2,128)} %param.19) | copy-start | bytes 196
  122.8 45.7 %copy-start.11 = (s32[1,8,2]{1,2,0:T(2,128)S(1)}, s32[1,8,2]{1,2,0:T(2,128)}, u32[]{:S(2)}) copy-start(s32[1,8,2]{1,2,0:T(2,128)} %param.18) | copy-start | bytes 196
  122.8 45.9 %copy-start.13 = (f32[1,8,2]{1,2,0:T(2,128)S(1)}, f32[1,8,2]{1,2,0:T(2,128)}, u32[]{:S(2)}) copy-start(f32[1,8,2]{1,2,0:T(2,128)} %param.20) | copy-start | bytes 196
  122.8 46.8 %copy-start.14 = (f32[1,8,2]{1,2,0:T(2,128)S(1)}, f32[1,8,2]{1,2,0:T(2,128)}, u32[]{:S(2)}) copy-start(f32[1,8,2]{1,2,0:T(2,128)} %param.16) | copy-start | bytes 196
  155.8 52.4 %all-to-all-start.1 = ((bf16[32,8,3584]{2,1,0:T(8,128)(2,1)}), bf16[32,8,3584]{2,1,0:T(8,128)(2,1)S(1)}, u32[]{:S(2)}, u32[]{:S(2)}) async-start(bf16[32,8,3584]{2,1,0:T(8,128)(2,1)} %fusion.1), calls=%async_computation.1 | async-start | bytes 3670016 | tf_op jit(solution)/shard_map/all_to_all | solution.py:52
  173.3 2.1 copy-start.1
  174.3 34.2 %copy-start.8 = (s32[1024]{0:T(1024)S(1)}, s32[1024]{0:T(1024)}, u32[]{:S(2)}) copy-start(s32[1024]{0:T(1024)} %pad_clamp_fusion.2) | copy-start | bytes 12292
  175.4 38.6 %collective-permute-start.1 = (bf16[1,8,3584]{2,1,0:T(8,128)(2,1)S(1)}, bf16[1,8,3584]{2,1,0:T(8,128)(2,1)S(1)}, u32[]{:S(2)}, u32[]{:S(2)}) collective-permute-start(bf16[1,8,3584]{2,1,0:T(8,128)(2,1)S(1)} %fusion.39), channel_id=1, source_target_pairs={{0,480},{32,0},{64,32},{96,64},{128,96},{160,128},{192,160},{224,1... | collective-permute-start | bytes 172040 | tf_op jit(solution)/shard_map/ppermute | solution.py:11
  208.4 0.8 copy-start.7
  209.6 21.4 %collective-permute-start = (bf16[1,8,3584]{2,1,0:T(8,128)(2,1)S(1)}, bf16[1,8,3584]{2,1,0:T(8,128)(2,1)S(1)}, u32[]{:S(2)}, u32[]{:S(2)}) collective-permute-start(bf16[1,8,3584]{2,1,0:T(8,128)(2,1)S(1)} %fusion.40), channel_id=1, source_target_pairs={{0,32},{32,64},{64,96},{96,128},{128,160},{160,192},{192,224},{224... | collective-permute-start | bytes 172040 | tf_op jit(solution)/shard_map/ppermute | solution.py:11
where the time goes:
time: 233 us; the launch traced here: 232 us
  waiting for transfers between devices  141 us (61%)
  starting transfers between devices  62.5 us (27%)
  local copies, waits for them, and re-layouts  10.5 us (5%)
  matrix products  10.4 us (4%)
  other arithmetic  6.71 us (3%)
    all_to_all x2, waiting for transfers between devices, send_back(): lax.all_to_all(partial_value, 'expert', split_axis=0, concat_axis=0, tile...  53.5 us
    all_to_all x1, waiting for transfers between devices, local(): lax.all_to_all(send_bwd, 'expert', split_axis=0, concat_axis=0, tiled=True)  38.4 us
    all_to_all x1, waiting for transfers between devices, local(): lax.all_to_all(send_fwd, 'expert', split_axis=0, concat_axis=0, tiled=True)  32.2 us
    all_to_all x2, starting transfers between devices, send_back(): lax.all_to_all(partial_value, 'expert', split_axis=0, concat_axis=0, tile...  26.1 us
    ppermute x2, waiting for transfers between devices, passed_along(): lax.ppermute(array, axis, [(i, (i + by) % peers) for i in range(peers)])  17.1 us
    ppermute x2, starting transfers between devices, passed_along(): lax.ppermute(array, axis, [(i, (i + by) % peers) for i in range(peers)])  16.6 us
    all_to_all x1, starting transfers between devices, local(): lax.all_to_all(send_fwd, 'expert', split_axis=0, concat_axis=0, tiled=True)  10.6 us
    all_to_all x1, starting transfers between devices, local(): lax.all_to_all(send_bwd, 'expert', split_axis=0, concat_axis=0, tiled=True)  9.18 us
  transfers between devices with their start and end apart: 6, of which 5 were waited for; matrix products, arithmetic and copies ran while one was open for 8% of the time, Pallas kernels for 0%

commit v1 on v0

v1 whole, which is shorter than its diff:
```python
import jax
import jax.numpy as jnp
from jax import lax
from jax.experimental import pallas as pl
from jax.experimental.pallas import tpu as pltpu
from jax.sharding import PartitionSpec as P

NX, NY, ROWS, D, HID = 4, 4, 8, 3584, 128
META = 128
HALF = D // 2
NC = 2
C = D // NC
KSTEP = 512
SUB = 256
BF, F32 = jnp.bfloat16, jnp.float32

Y_MINUS, Y_PLUS, Y_FAR_A, Y_FAR_B, X_MINUS, X_PLUS, X_FAR, SIB = 0, 1, 2, 3, 4, 8, 12, 16
N_GATHER = 20
C_SIB, C_FAR_P, C_FAR_M, C_ONE_P, C_ONE_M, C_TWO_P, C_TWO_M, C_YFAR, C_Y_P, C_Y_M, C_OWN = range(11)
N_COMBINE = 11


def dot(a, b):
    return lax.dot_general(a, b, (((1,), (0,)), ((), ())), preferred_element_type=F32)


def dot_t(a, b):
    return lax.dot_general(a, b, (((1,), (1,)), ((), ())), preferred_element_type=F32)


def routing_lanes(route, slot, weight, first):
    lane = lax.broadcasted_iota(jnp.int32, (ROWS, META), 1) - first
    square = (ROWS, ROWS)
    same = lax.broadcasted_iota(jnp.int32, square, 0) == lax.broadcasted_iota(jnp.int32, square, 1)

    def column(values, k):
        return jnp.sum(jnp.where(same, values[k : k + 1, :].astype(F32), 0.0), axis=1, keepdims=True)

    total = jnp.zeros((ROWS, META), F32)
    for k in range(2):
        expert = column(route, k).astype(jnp.int32)
        w = column(weight, k)
        hi = w.astype(BF).astype(F32)
        mid = (w - hi).astype(BF).astype(F32)
        low = w - hi - mid
        place = column(slot, k) + 1.0
        for i, part in enumerate((hi, mid, low, place)):
            total = total + jnp.where(lane == expert + 4 * i, part, 0.0)
    return total


def kernel(
    act, route_f, slot_f, weight_f, grad, route_b, slot_b, weight_b, saved_gate, saved_up, w_gate, w_up, w_down,
    out_f, out_b,
    xf, xb, wcat, wd, saved, ri, wi,
    part_f, part_b, sib_s, sib_r, far_s, far_r, near_s, near_r, yfar_s, yfar_r, ynear_s, ynear_r, own_s, own_r, base_r,
    gs, gr, cs, cr, bs, br, ls,
):
    sec = lax.axis_index("section")
    ex = lax.axis_index("expert")
    nsec = lax.axis_size("section")
    x, y, c = ex // (NY * 2), (ex // 2) % NY, ex % 2
    oc = 1 - c
    xs = [(x + i) % NX for i in range(NX)]
    ys = [(y + i) % NY for i in range(NY)]
    to = [(sec + 1) % nsec, (sec + nsec - 1) % nsec]

    def dev(xi, yi, ci, s=sec):
        return (s, xi * (NY * 2) + yi * 2 + ci)

    def copy(src, dst, send, recv, device):
        return pltpu.make_async_remote_copy(
            src_ref=src, dst_ref=dst, send_sem=send, recv_sem=recv, device_id=device,
            device_id_type=pl.DeviceIdType.MESH,
        )

    sib = dev(x, y, oc)
    x_to = {1: dev(xs[1], y, c), -1: dev(xs[3], y, c)}
    y_to = {1: dev(x, ys[1], c), -1: dev(x, ys[3], c)}
    gathered = (xf, xb)
    widths = (D + META, D)
    parts = (part_f, part_b)
    outs = (out_f, out_b)

    loads = [
        pltpu.make_async_copy(act.at[0], xf.at[x, y, c, :, pl.ds(0, D)], ls.at[0]),
        pltpu.make_async_copy(grad.at[0], xb.at[x, y, c], ls.at[1]),
        pltpu.make_async_copy(route_f.at[0], ri.at[0], ls.at[2]),
        pltpu.make_async_copy(slot_f.at[0], ri.at[1], ls.at[3]),
        pltpu.make_async_copy(route_b.at[0], ri.at[2], ls.at[4]),
        pltpu.make_async_copy(slot_b.at[0], ri.at[3], ls.at[5]),
        pltpu.make_async_copy(weight_f.at[0], wi.at[0], ls.at[6]),
        pltpu.make_async_copy(weight_b.at[0], wi.at[1], ls.at[7]),
        pltpu.make_async_copy(w_gate.at[0], wcat.at[:, pl.ds(0, HID)], ls.at[8]),
        pltpu.make_async_copy(w_up.at[0], wcat.at[:, pl.ds(HID, HID)], ls.at[9]),
        pltpu.make_async_copy(w_down.at[0], wd, ls.at[10]),
        pltpu.make_async_copy(saved_gate.at[0], saved.at[:, :, pl.ds(0, HID)], ls.at[11]),
        pltpu.make_async_copy(saved_up.at[0], saved.at[:, :, pl.ds(HID, HID)], ls.at[12]),
    ]
    for load in loads:
        load.start()

    barrier = pltpu.get_barrier_semaphore()
    partners = [sib, x_to[1], x_to[-1], y_to[1], y_to[-1]]
    partners += [dev(x, yi, c, s) for s in to for yi in (ys[0], ys[1], ys[3])]
    for partner in partners:
        pl.semaphore_signal(barrier, inc=1, device_id=partner, device_id_type=pl.DeviceIdType.MESH)
    for load in loads[2:8]:
        load.wait()
    lanes = routing_lanes(ri[0], ri[1], wi[0], 0) + routing_lanes(ri[2], ri[3], wi[1], 16)
    for load in loads[0:2]:
        load.wait()
    xf[x, y, c, :, pl.ds(D, META)] = lanes.astype(BF)
    pl.semaphore_wait(barrier, len(partners))

    def g_copy(p, ref, sem, device):
        return copy(ref, ref, gs.at[p, sem], gr.at[p, sem], device)

    def block(p, xi, yi):
        return gathered[p].at[xi, yi, c]

    def y_half(p, yi, half):
        cols = pl.ds(0, HALF) if half == 0 else pl.ds(HALF, widths[p] - HALF)
        return gathered[p].at[x, yi, c, :, cols]

    def sib_line(p, i):
        return g_copy(p, gathered[p].at[xs[i], :, c], SIB + i, sib)

    def send_x(p, r):
        g_copy(p, block(p, x, ys[r]), X_MINUS + r, x_to[1]).start()
        g_copy(p, block(p, x, ys[r]), X_PLUS + r, x_to[-1]).start()

    def x_in(p, r):
        g_copy(p, block(p, xs[3], ys[r]), X_MINUS + r, x_to[1]).wait_recv()
        if r in (0, 1):
            g_copy(p, block(p, xs[3], ys[r]), X_FAR + r, x_to[1]).start()
        g_copy(p, block(p, xs[1], ys[r]), X_PLUS + r, x_to[-1]).wait_recv()
        if r in (2, 3):
            g_copy(p, block(p, xs[1], ys[r]), X_FAR + r, x_to[-1]).start()

    def own_out(p):
        g_copy(p, block(p, x, y), Y_MINUS, y_to[1]).start()
        g_copy(p, block(p, x, y), Y_PLUS, y_to[-1]).start()
        send_x(p, 0)

    def y_pass(p):
        g_copy(p, block(p, x, ys[3]), Y_MINUS, y_to[1]).wait_recv()
        g_copy(p, y_half(p, ys[3], 0), Y_FAR_A, y_to[1]).start()
        send_x(p, 3)
        g_copy(p, block(p, x, ys[1]), Y_PLUS, y_to[-1]).wait_recv()
        g_copy(p, y_half(p, ys[1], 1), Y_FAR_B, y_to[-1]).start()
        send_x(p, 1)
        g_copy(p, y_half(p, ys[2], 0), Y_FAR_A, y_to[1]).wait_recv()
        g_copy(p, y_half(p, ys[2], 1), Y_FAR_B, y_to[-1]).wait_recv()
        send_x(p, 2)
        sib_line(p, 0).start()

    def x_pass(p):
        for r in (3, 1, 2):
            x_in(p, r)
        sib_line(p, 3).start()
        sib_line(p, 1).start()

    def x_far(p):
        for r in range(4):
            g_copy(p, block(p, xs[2], ys[r]), X_FAR + r, x_to[1]).wait_recv()
        sib_line(p, 2).start()

    def sib_in(p):
        for i in range(4):
            g_copy(p, gathered[p].at[xs[i], :, oc], SIB + i, sib).wait_recv()

    def gather_sent(p):
        g_copy(p, block(p, x, y), Y_MINUS, y_to[1]).wait_send()
        g_copy(p, block(p, x, y), Y_PLUS, y_to[-1]).wait_send()
        g_copy(p, y_half(p, ys[3], 0), Y_FAR_A, y_to[1]).wait_send()
        g_copy(p, y_half(p, ys[1], 1), Y_FAR_B, y_to[-1]).wait_send()
        for r in range(4):
            g_copy(p, block(p, x, ys[r]), X_MINUS + r, x_to[1]).wait_send()
            g_copy(p, block(p, x, ys[r]), X_PLUS + r, x_to[-1]).wait_send()
            g_copy(p, block(p, xs[3], ys[r]), X_FAR + r, x_to[1]).wait_send()
            sib_line(p, r).wait_send()

    def base_copy(p):
        src = gathered[p].at[x, y, c, :, pl.ds(0, D)]
        return copy(src, base_r.at[p], bs.at[p], br.at[p], dev(x, y, c, to[p]))

    def weights_of(p):
        meta = xf[:, :, :, :, pl.ds(D, META)].reshape(NX * NY * 2 * ROWS, META).astype(F32)
        lane = lax.broadcasted_iota(jnp.int32, meta.shape, 1) - (16 * p + x)
        picked = (lane == 0) | (lane == 4) | (lane == 8)
        weight = jnp.sum(jnp.where(picked, meta, 0.0), axis=1, keepdims=True)
        place = jnp.sum(jnp.where(lane == 12, meta, 0.0), axis=1, keepdims=True)
        return weight, place

    def rows_of(ref, k):
        return ref[:, :, :, :, pl.ds(k, KSTEP)].reshape(NX * NY * 2 * ROWS, KSTEP)

    def put(p, lo, value, weight):
        k, off = lo // C, lo % C
        value = (value * weight).reshape(NX, NY, 2, ROWS, SUB)
        parts[p][k, :, :, :, :, pl.ds(off, SUB)] = value
        sib_s[p, k, :, :, :, :, pl.ds(off, SUB)] = value.astype(BF)

    def c_copy(p, k, src, dst, sem, device):
        return copy(src, dst, cs.at[p, k, sem], cr.at[p, k, sem], device)

    def sib_out(p, k):
        return c_copy(p, k, sib_s.at[p, k, :, :, oc], sib_r.at[p, k], C_SIB, sib)

    def forward():
        acc = jnp.zeros((256, 2 * HID), F32)
        for k in range(0, D, KSTEP):
            acc = acc + dot(rows_of(xf, k), wcat[pl.ds(k, KSTEP), :])
        g, u = acc[:, :HID], acc[:, HID:]
        h = (g / (1.0 + jnp.exp(-g)) * u).astype(BF)
        weight, _ = weights_of(0)
        for k in range(NC):
            for lo in range(k * C, (k + 1) * C, SUB):
                put(0, lo, dot(h, wd[:, pl.ds(lo, SUB)]), weight)
            sib_out(0, k).start()

    def backward():
        dh = jnp.zeros((256, HID), F32)
        for k in range(0, D, KSTEP):
            dh = dh + dot_t(rows_of(xb, k), wd[:, pl.ds(k, KSTEP)])
        weight, place = weights_of(1)
        row = lax.broadcasted_iota(jnp.int32, (256, 1), 0)
        target = (row - row % 8).astype(F32) + place - 1.0
        target = jnp.where(place > 0.5, target, -1.0)
        col = lax.broadcasted_iota(jnp.int32, (256, 256), 1).astype(F32)
        pick = jnp.where(col == target, 1.0, 0.0).astype(BF)
        kept = dot(pick, saved[...].reshape(256, 2 * HID))
        a, b = kept[:, :HID], kept[:, HID:]
        sigma = 1.0 / (1.0 + jnp.exp(-a))
        dg = dh * b * (sigma * (1.0 + a * (1.0 - sigma)))
        du = dh * a * sigma
        dgu = jnp.concatenate([dg.astype(BF), du.astype(BF)], axis=1)
        for k in range(NC):
            for lo in range(k * C, (k + 1) * C, SUB):
                put(1, lo, dot_t(dgu, wcat[pl.ds(lo, SUB), :]), weight)
            sib_out(1, k).start()

    lower, upper = pl.ds(0, 2), pl.ds(2, 2)

    def both(p, k, xi, rows):
        return parts[p][k, xi, rows, c] + sib_r[p, k, xi, rows].astype(F32)

    def far(p, k, d):
        i = 0 if d > 0 else 1
        return c_copy(p, k, far_s.at[p, k, i], far_r.at[p, k, i], C_FAR_P + i, x_to[d])

    def near(p, k, d, rows, sem):
        i = 0 if d > 0 else 1
        return c_copy(p, k, near_s.at[p, k, i, rows], near_r.at[p, k, i, rows], sem + i, x_to[d])

    def x_one(p, k):
        sib_out(p, k).wait_recv()
        far_s[p, k, 0] = both(p, k, xs[2], lower).astype(BF)
        far(p, k, 1).start()
        far_s[p, k, 1] = both(p, k, xs[2], upper).astype(BF)
        far(p, k, -1).start()
        near_s[p, k, 0, upper] = both(p, k, xs[1], upper).astype(BF)
        near(p, k, 1, upper, C_ONE_P).start()
        near_s[p, k, 1, lower] = both(p, k, xs[3], lower).astype(BF)
        near(p, k, -1, lower, C_ONE_P).start()

    def x_two(p, k):
        far(p, k, 1).wait_recv()
        near_s[p, k, 0, lower] = (both(p, k, xs[1], lower) + far_r[p, k, 0].astype(F32)).astype(BF)
        near(p, k, 1, lower, C_TWO_P).start()
        far(p, k, -1).wait_recv()
        near_s[p, k, 1, upper] = (both(p, k, xs[3], upper) + far_r[p, k, 1].astype(F32)).astype(BF)
        near(p, k, -1, upper, C_TWO_P).start()

    def line(p, k, yi):
        mine = parts[p][k, x, yi, c] + sib_r[p, k, x, yi].astype(F32)
        return mine + near_r[p, k, 0, yi].astype(F32) + near_r[p, k, 1, yi].astype(F32)

    def y_far(p, k):
        return c_copy(p, k, yfar_s.at[p, k], yfar_r.at[p, k], C_YFAR, y_to[1 if k % 2 == 0 else -1])

    def y_near(p, k, d):
        i = 0 if d > 0 else 1
        device = dev(x, ys[1] if d > 0 else ys[3], c, to[p])
        return c_copy(p, k, ynear_s.at[p, k, i], ynear_r.at[p, k, i], C_Y_P + i, device)

    def y_own(p, k):
        return c_copy(p, k, own_s.at[p, k], own_r.at[p, k], C_OWN, dev(x, y, c, to[p]))

    def y_one(p, k):
        near(p, k, 1, upper, C_ONE_P).wait_recv()
        near(p, k, -1, lower, C_ONE_P).wait_recv()
        near(p, k, 1, lower, C_TWO_P).wait_recv()
        near(p, k, -1, upper, C_TWO_P).wait_recv()
        d = 1 if k % 2 == 0 else -1
        yfar_s[p, k] = line(p, k, ys[2]).astype(BF)
        y_far(p, k).start()
        ynear_s[p, k, 1 if d > 0 else 0] = line(p, k, ys[3] if d > 0 else ys[1]).astype(BF)
        y_near(p, k, -d).start()
        own_s[p, k] = line(p, k, y).astype(BF)
        y_own(p, k).start()

    def y_two(p, k):
        d = 1 if k % 2 == 0 else -1
        y_far(p, k).wait_recv()
        merged = line(p, k, ys[1] if d > 0 else ys[3]) + yfar_r[p, k].astype(F32)
        ynear_s[p, k, 0 if d > 0 else 1] = merged.astype(BF)
        y_near(p, k, d).start()

    def finish(p, k):
        y_own(p, k).wait_recv()
        y_near(p, k, 1).wait_recv()
        y_near(p, k, -1).wait_recv()
        cols = pl.ds(k * C, C)
        total = base_r[p, :, cols].astype(F32) + own_r[p, k].astype(F32)
        total = total + ynear_r[p, k, 0].astype(F32) + ynear_r[p, k, 1].astype(F32)
        outs[p][0, :, cols] = total.astype(BF)

    def combine_sent(p, k):
        sib_out(p, k).wait_send()
        for d in (1, -1):
            far(p, k, d).wait_send()
            near(p, k, d, lower, C_ONE_P if d < 0 else C_TWO_P).wait_send()
            near(p, k, d, upper, C_ONE_P if d > 0 else C_TWO_P).wait_send()
            y_near(p, k, d).wait_send()
        y_far(p, k).wait_send()
        y_own(p, k).wait_send()

    own_out(0)
    own_out(1)
    x_in(0, 0)
    y_pass(0)
    base_copy(0).start()
    base_copy(1).start()
    x_in(1, 0)
    y_pass(1)
    x_pass(0)
    x_far(0)
    x_pass(1)
    for load in loads[8:11]:
        load.wait()
    sib_in(0)
    forward()
    x_far(1)
    for k in range(NC):
        x_one(0, k)
    for k in range(NC):
        x_two(0, k)
    for load in loads[11:13]:
        load.wait()
    sib_in(1)
    backward()
    for k in range(NC):
        y_one(0, k)
    for k in range(NC):
        x_one(1, k)
    for k in range(NC):
        y_two(0, k)
    for k in range(NC):
        x_two(1, k)
    base_copy(0).wait_recv()
    for k in range(NC):
        finish(0, k)
    for k in range(NC):
        y_one(1, k)
    for k in range(NC):
        y_two(1, k)
    base_copy(1).wait_recv()
    for k in range(NC):
        finish(1, k)
    for p in range(2):
        gather_sent(p)
        base_copy(p).wait_send()
        for k in range(NC):
            combine_sent(p, k)


def local(*args):
    args = [a.transpose(0, 2, 1) if a.shape[-1] == 2 else a for a in args]
    out = jax.ShapeDtypeStruct((1, ROWS, D), BF)
    vm = pltpu.VMEM
    return pl.pallas_call(
        kernel,
        out_shape=(out, out),
        in_specs=[pl.BlockSpec(memory_space=pltpu.HBM)] * 13,
        out_specs=[pl.BlockSpec(memory_space=pltpu.VMEM)] * 2,
        scratch_shapes=[
            vm((NX, NY, 2, ROWS, D + META), BF),
            vm((NX, NY, 2, ROWS, D), BF),
            vm((D, 2 * HID), BF),
            vm((HID, D), BF),
            vm((32, 8, 2 * HID), BF),
            vm((4, 2, ROWS), jnp.int32),
            vm((2, 2, ROWS), F32),
            vm((NC, NX, NY, 2, ROWS, C), F32),
            vm((NC, NX, NY, 2, ROWS, C), F32),
            vm((2, NC, NX, NY, 2, ROWS, C), BF),
            vm((2, NC, NX, NY, ROWS, C), BF),
            vm((2, NC, 2, 2, ROWS, C), BF),
            vm((2, NC, 2, 2, ROWS, C), BF),
            vm((2, NC, 2, 4, ROWS, C), BF),
            vm((2, NC, 2, 4, ROWS, C), BF),
            vm((2, NC, ROWS, C), BF),
            vm((2, NC, ROWS, C), BF),
            vm((2, NC, 2, ROWS, C), BF),
            vm((2, NC, 2, ROWS, C), BF),
            vm((2, NC, ROWS, C), BF),
            vm((2, NC, ROWS, C), BF),
            vm((2, ROWS, D), BF),
            pltpu.SemaphoreType.DMA((2, N_GATHER)),
            pltpu.SemaphoreType.DMA((2, N_GATHER)),
            pltpu.SemaphoreType.DMA((2, NC, N_COMBINE)),
            pltpu.SemaphoreType.DMA((2, NC, N_COMBINE)),
            pltpu.SemaphoreType.DMA((2,)),
            pltpu.SemaphoreType.DMA((2,)),
            pltpu.SemaphoreType.DMA((13,)),
        ],
        compiler_params=pltpu.CompilerParams(
            collective_id=0, has_side_effects=True, vmem_limit_bytes=48 * 1024 * 1024
        ),
        cost_estimate=pl.CostEstimate(flops=1_500_000_000, bytes_accessed=4_000_000, transcendentals=70_000),
    )(*args)


def solution(mesh):
    tokens = P("section", "expert", None)
    saved = P("section", None, None, "expert")
    cols = P("section", None, "expert")
    in_specs = (tokens,) * 8 + (saved, saved, cols, cols, tokens)
    return jax.shard_map(local, mesh=mesh, in_specs=in_specs, out_specs=(tokens, tokens), check_vma=False)
```

time: 233 us -> 77.7 us (0.33)
  waiting for transfers between devices: 141 us -> 0 us
  Pallas kernels: 0 us -> 67.7 us
  starting transfers between devices: 62.5 us -> 0 us
  matrix products: 10.4 us -> 0 us
  other arithmetic: 6.71 us -> 0 us
    all_to_all x4 -> x0, waiting for transfers between devices: 124 us -> none  [the longest x2 53.5 us: send_back(): lax.all_to_all(partial_value, 'expert', split_axis=0, concat_axis=0, tile...]
    pallas_call x0 -> x1, Pallas kernels: none -> 67.7 us  [local(): pl.pallas_call(kernel, out_shape=(out, out), in_specs=[pl.BlockSpec(memor...]
    all_to_all x4 -> x0, starting transfers between devices: 45.9 us -> none  [the longest x2 26.1 us: send_back(): lax.all_to_all(partial_value, 'expert', split_axis=0, concat_axis=0, tile...]
    ppermute x2 -> x0, waiting for transfers between devices: 17.1 us -> none  [passed_along(): lax.ppermute(array, axis, [(i, (i + by) % peers) for i in range(peers)])]
    ppermute x2 -> x0, starting transfers between devices: 16.6 us -> none  [passed_along(): lax.ppermute(array, axis, [(i, (i + by) % peers) for i in range(peers)])]
    dot_general x5 -> x0, matrix products: 10.4 us -> none  [the longest x1 3.62 us: forward_local(): jnp.dot(hidden, down_rows, preferred_element_type=jnp.float32)]
    unnamed x32 -> x28, local copies, waits for them, and re-layouts: 1.66 us -> 8.81 us
    gather x6 -> x0, local copies, waits for them, and re-layouts: 4.2 us -> none  [the longest x2 2.42 us: outgoing(): tokens[position]]
  transfers between devices with their start and end apart: 6 -> 0, of which waited for: 5 -> 0; matrix products, arithmetic and copies ran while one was open for 8% -> 0% of each run, Pallas kernels for 0% -> 0%
where the time goes in v1:
time: 77.7 us; the launch traced here: 77.2 us
  Pallas kernels  67.7 us (87%)
  local copies, waits for them, and re-layouts  8.81 us (11%)
    pallas_call x1, Pallas kernels, local(): pl.pallas_call(kernel, out_shape=(out, out), in_specs=[pl.BlockSpec(memor...  67.7 us
    unnamed x28, local copies, waits for them, and re-layouts  8.81 us

profile of v1, /device:TPU:8, one launch (start us, length us, event | category | flops | bytes accessed | tf_op | source)
XLA Modules:
  0.0 77.2 jit_solution(1948242003400826892)
XLA Ops:
  0.6 0.0 copy-start.12
  0.6 0.0 copy-start.10
  0.7 0.0 copy-start.11
  0.7 0.0 copy-start.8
  0.7 0.0 copy-start.9
  0.7 0.0 copy-start.7
  0.7 0.6 copy-done.12
  1.3 0.0 copy-done.10
  1.3 0.0 copy-done.11
  1.3 0.0 copy-done.8
  1.4 0.0 copy-done.9
  1.4 0.0 copy-done.7
  1.4 0.0 copy-start
  1.4 1.2 %copy-done = bf16[1,3584,128]{2,1,0:T(8,128)(2,1)S(1)} copy-done((bf16[1,3584,128]{2,1,0:T(8,128)(2,1)S(1)}, bf16[1,3584,128]{2,1,0:T(8,128)(2,1)}, u32[]{:S(2)}) %copy-start) | copy-done | bytes 917528
  2.6 0.0 copy-start.1
  2.6 1.2 %copy-done.1 = bf16[1,3584,128]{2,1,0:T(8,128)(2,1)S(1)} copy-done((bf16[1,3584,128]{2,1,0:T(8,128)(2,1)S(1)}, bf16[1,3584,128]{2,1,0:T(8,128)(2,1)}, u32[]{:S(2)}) %copy-start.1) | copy-done | bytes 917528
  3.8 0.0 copy-start.2
  3.8 1.2 %copy-done.2 = bf16[1,128,3584]{2,1,0:T(8,128)(2,1)S(1)} copy-done((bf16[1,128,3584]{2,1,0:T(8,128)(2,1)S(1)}, bf16[1,128,3584]{2,1,0:T(8,128)(2,1)}, u32[]{:S(2)}) %copy-start.2) | copy-done | bytes 917528
  4.9 0.0 copy-start.3
  4.9 0.8 %copy-done.3 = bf16[1,32,8,128]{3,2,1,0:T(8,128)(2,1)S(1)} copy-done((bf16[1,32,8,128]{3,2,1,0:T(8,128)(2,1)S(1)}, bf16[1,32,8,128]{3,2,1,0:T(8,128)(2,1)}, u32[]{:S(2)}) %copy-start.3) | copy-done | bytes 65560
  5.8 0.0 copy-start.4
  5.8 0.8 %copy-done.4 = bf16[1,32,8,128]{3,2,1,0:T(8,128)(2,1)S(1)} copy-done((bf16[1,32,8,128]{3,2,1,0:T(8,128)(2,1)S(1)}, bf16[1,32,8,128]{3,2,1,0:T(8,128)(2,1)}, u32[]{:S(2)}) %copy-start.4) | copy-done | bytes 65560
  6.6 0.0 copy-start.5
  6.6 0.8 %copy-done.5 = bf16[1,8,3584]{2,1,0:T(8,128)(2,1)S(1)} copy-done((bf16[1,8,3584]{2,1,0:T(8,128)(2,1)S(1)}, bf16[1,8,3584]{2,1,0:T(8,128)(2,1)}, u32[]{:S(2)}) %copy-start.5) | copy-done | bytes 57368
  7.4 0.0 copy-start.6
  7.4 0.8 %copy-done.6 = bf16[1,8,3584]{2,1,0:T(8,128)(2,1)S(1)} copy-done((bf16[1,8,3584]{2,1,0:T(8,128)(2,1)S(1)}, bf16[1,8,3584]{2,1,0:T(8,128)(2,1)}, u32[]{:S(2)}) %copy-start.6) | copy-done | bytes 57368
  8.3 67.7 %shard_map.140 = (bf16[1,8,3584]{2,1,0:T(8,128)(2,1)S(1)}, bf16[1,8,3584]{2,1,0:T(8,128)(2,1)S(1)}) custom-call(bf16[1,8,3584]{2,1,0:T(8,128)(2,1)S(1)} %copy-done.5, s32[1,2,8]{2,1,0:T(2,128)S(1)} %bitcast.6, s32[1,2,8]{2,1,0:T(2,128)S(1)} %bitcast.7, f32[1,2,8]{2,1,0:T(2,128)S(1)} %bitcast.8, bf16[1,8,3584]{2,1,0:T(8,128)(2,1)S(1)} %copy-done.6, ...), custom_call_target="tpu_custom_call" | custom-call | flops 1500000000 | bytes 4000000 | tf_op jit(solution)/shard_map/pallas_call | solution.py:383
  76.0 0.6 copy.17
  76.6 0.6 copy.18
Async XLA Ops:
  0.6 0.7 copy-start.12
  0.6 0.7 copy-start.10
  0.7 0.7 copy-start.11
  0.7 0.7 copy-start.8
  0.7 0.7 copy-start.9
  0.7 0.7 copy-start.7
  1.4 1.2 %copy-start = (bf16[1,3584,128]{2,1,0:T(8,128)(2,1)S(1)}, bf16[1,3584,128]{2,1,0:T(8,128)(2,1)}, u32[]{:S(2)}) copy-start(bf16[1,3584,128]{2,1,0:T(8,128)(2,1)} %w_gate.1) | copy-start | bytes 2752516
  2.6 1.2 %copy-start.1 = (bf16[1,3584,128]{2,1,0:T(8,128)(2,1)S(1)}, bf16[1,3584,128]{2,1,0:T(8,128)(2,1)}, u32[]{:S(2)}) copy-start(bf16[1,3584,128]{2,1,0:T(8,128)(2,1)} %w_up.1) | copy-start | bytes 2752516
  3.8 1.2 %copy-start.2 = (bf16[1,128,3584]{2,1,0:T(8,128)(2,1)S(1)}, bf16[1,128,3584]{2,1,0:T(8,128)(2,1)}, u32[]{:S(2)}) copy-start(bf16[1,128,3584]{2,1,0:T(8,128)(2,1)} %w_down.1) | copy-start | bytes 2752516
  4.9 0.8 %copy-start.3 = (bf16[1,32,8,128]{3,2,1,0:T(8,128)(2,1)S(1)}, bf16[1,32,8,128]{3,2,1,0:T(8,128)(2,1)}, u32[]{:S(2)}) copy-start(bf16[1,32,8,128]{3,2,1,0:T(8,128)(2,1)} %saved_gate.1) | copy-start | bytes 196612
  5.8 0.8 %copy-start.4 = (bf16[1,32,8,128]{3,2,1,0:T(8,128)(2,1)S(1)}, bf16[1,32,8,128]{3,2,1,0:T(8,128)(2,1)}, u32[]{:S(2)}) copy-start(bf16[1,32,8,128]{3,2,1,0:T(8,128)(2,1)} %saved_up.1) | copy-start | bytes 196612
  6.6 0.8 %copy-start.5 = (bf16[1,8,3584]{2,1,0:T(8,128)(2,1)S(1)}, bf16[1,8,3584]{2,1,0:T(8,128)(2,1)}, u32[]{:S(2)}) copy-start(bf16[1,8,3584]{2,1,0:T(8,128)(2,1)} %act.1) | copy-start | bytes 172036
  7.4 0.8 %copy-start.6 = (bf16[1,8,3584]{2,1,0:T(8,128)(2,1)S(1)}, bf16[1,8,3584]{2,1,0:T(8,128)(2,1)}, u32[]{:S(2)}) copy-start(bf16[1,8,3584]{2,1,0:T(8,128)(2,1)} %grad.1) | copy-start | bytes 172036

commit v2 on v1

--- a/solution.py
+++ b/solution.py
@@ -5,14 +5,17 @@
 from jax.experimental.pallas import tpu as pltpu
 from jax.sharding import PartitionSpec as P
 
-NX, NY, ROWS, D, HID = 4, 4, 8, 3584, 128
+NX, NY, NZ, ROWS, D, HID = 4, 4, 8, 8, 3584, 128
 META = 128
 HALF = D // 2
-NC = 2
+NC = 4
 C = D // NC
 KSTEP = 512
-SUB = 256
+SUB = 896
 BF, F32 = jnp.bfloat16, jnp.float32
+X_DIRECT, Y_DIRECT = (2,), False
+BASE_AT = (0, 0)
+FAR_DIRECT, YFAR_DIRECT = False, True
 
 Y_MINUS, Y_PLUS, Y_FAR_A, Y_FAR_B, X_MINUS, X_PLUS, X_FAR, SIB = 0, 1, 2, 3, 4, 8, 12, 16
 N_GATHER = 20
@@ -54,7 +57,7 @@
     out_f, out_b,
     xf, xb, wcat, wd, saved, ri, wi,
     part_f, part_b, sib_s, sib_r, far_s, far_r, near_s, near_r, yfar_s, yfar_r, ynear_s, ynear_r, own_s, own_r, base_r,
-    gs, gr, cs, cr, bs, br, ls,
+    hid, scale, z_sem, gs, gr, cs, cr, bs, br, ls,
 ):
     sec = lax.axis_index("section")
     ex = lax.axis_index("expert")
@@ -101,17 +104,49 @@
         load.start()
 
     barrier = pltpu.get_barrier_semaphore()
-    partners = [sib, x_to[1], x_to[-1], y_to[1], y_to[-1]]
-    partners += [dev(x, yi, c, s) for s in to for yi in (ys[0], ys[1], ys[3])]
-    for partner in partners:
-        pl.semaphore_signal(barrier, inc=1, device_id=partner, device_id_type=pl.DeviceIdType.MESH)
+    zi = sec % NZ
+    near_devices = [sib, x_to[1], x_to[-1], dev(xs[2], y, c), y_to[1], y_to[-1], dev(x, ys[2], c)]
+    after = [dev(x, yi, c, to[0]) for yi in ys]
+    before = [dev(x, yi, c, to[1]) for yi in ys]
+
+    def tell(sem, devices):
+        for device in devices:
+            pl.semaphore_signal(sem, inc=1, device_id=device, device_id_type=pl.DeviceIdType.MESH)
+
+    tell(barrier, near_devices)
+
+    @pl.when(zi < NZ - 1)
+    def _():
+        tell(barrier, after)
+
+    @pl.when(zi == 0)
+    def _():
+        tell(barrier, before)
+
     for load in loads[2:8]:
         load.wait()
     lanes = routing_lanes(ri[0], ri[1], wi[0], 0) + routing_lanes(ri[2], ri[3], wi[1], 16)
     for load in loads[0:2]:
         load.wait()
     xf[x, y, c, :, pl.ds(D, META)] = lanes.astype(BF)
-    pl.semaphore_wait(barrier, len(partners))
+    def await_by_z(sem, first, middle, last):
+        for here, amount in ((zi == 0, first), ((zi > 0) & (zi < NZ - 1), middle), (zi == NZ - 1, last)):
+            if amount:
+
+                @pl.when(here)
+                def _():
+                    pl.semaphore_wait(sem, amount)
+
+    near_count = len(near_devices)
+    await_by_z(barrier, near_count, near_count + NY, near_count + 2 * NY)
+
+    @pl.when(zi > 0)
+    def _():
+        tell(z_sem, before)
+
+    @pl.when(zi == NZ - 1)
+    def _():
+        tell(z_sem, after)
 
     def g_copy(p, ref, sem, device):
         return copy(ref, ref, gs.at[p, sem], gr.at[p, sem], device)
@@ -129,35 +164,34 @@
     def send_x(p, r):
         g_copy(p, block(p, x, ys[r]), X_MINUS + r, x_to[1]).start()
         g_copy(p, block(p, x, ys[r]), X_PLUS + r, x_to[-1]).start()
+        if r in X_DIRECT:
+            g_copy(p, block(p, x, ys[r]), X_FAR + r, dev(xs[2], y, c)).start()
 
     def x_in(p, r):
         g_copy(p, block(p, xs[3], ys[r]), X_MINUS + r, x_to[1]).wait_recv()
-        if r in (0, 1):
+        if r in (0, 1) and r not in X_DIRECT:
             g_copy(p, block(p, xs[3], ys[r]), X_FAR + r, x_to[1]).start()
         g_copy(p, block(p, xs[1], ys[r]), X_PLUS + r, x_to[-1]).wait_recv()
-        if r in (2, 3):
+        if r in (2, 3) and r not in X_DIRECT:
             g_copy(p, block(p, xs[1], ys[r]), X_FAR + r, x_to[-1]).start()
 
-    def own_out(p):
+    def own_y(p):
         g_copy(p, block(p, x, y), Y_MINUS, y_to[1]).start()
         g_copy(p, block(p, x, y), Y_PLUS, y_to[-1]).start()
-        send_x(p, 0)
-
-    def y_pass(p):
-        g_copy(p, block(p, x, ys[3]), Y_MINUS, y_to[1]).wait_recv()
-        g_copy(p, y_half(p, ys[3], 0), Y_FAR_A, y_to[1]).start()
-        send_x(p, 3)
-        g_copy(p, block(p, x, ys[1]), Y_PLUS, y_to[-1]).wait_recv()
-        g_copy(p, y_half(p, ys[1], 1), Y_FAR_B, y_to[-1]).start()
-        send_x(p, 1)
+
+    def y_in(p, d):
+        i, r, sem, far_sem = (0, 3, Y_MINUS, Y_FAR_A) if d > 0 else (1, 1, Y_PLUS, Y_FAR_B)
+        g_copy(p, block(p, x, ys[r]), sem, y_to[d]).wait_recv()
+        g_copy(p, y_half(p, ys[r], i), far_sem, y_to[d]).start()
+        send_x(p, r)
+
+    def y_last(p):
         g_copy(p, y_half(p, ys[2], 0), Y_FAR_A, y_to[1]).wait_recv()
         g_copy(p, y_half(p, ys[2], 1), Y_FAR_B, y_to[-1]).wait_recv()
         send_x(p, 2)
         sib_line(p, 0).start()
 
-    def x_pass(p):
-        for r in (3, 1, 2):
-            x_in(p, r)
+    def sib_near(p):
         sib_line(p, 3).start()
         sib_line(p, 1).start()
 
@@ -181,6 +215,9 @@
             g_copy(p, block(p, xs[3], ys[r]), X_FAR + r, x_to[1]).wait_send()
             sib_line(p, r).wait_send()
 
+    def z_ready():
+        await_by_z(z_sem, 2 * NY, NY, 0)
+
     def base_copy(p):
         src = gathered[p].at[x, y, c, :, pl.ds(0, D)]
         return copy(src, base_r.at[p], bs.at[p], br.at[p], dev(x, y, c, to[p]))
@@ -208,19 +245,15 @@
     def sib_out(p, k):
         return c_copy(p, k, sib_s.at[p, k, :, :, oc], sib_r.at[p, k], C_SIB, sib)
 
-    def forward():
+    def hidden_f():
         acc = jnp.zeros((256, 2 * HID), F32)
         for k in range(0, D, KSTEP):
             acc = acc + dot(rows_of(xf, k), wcat[pl.ds(k, KSTEP), :])
         g, u = acc[:, :HID], acc[:, HID:]
-        h = (g / (1.0 + jnp.exp(-g)) * u).astype(BF)
-        weight, _ = weights_of(0)
-        for k in range(NC):
-            for lo in range(k * C, (k + 1) * C, SUB):
-                put(0, lo, dot(h, wd[:, pl.ds(lo, SUB)]), weight)
-            sib_out(0, k).start()
-
-    def backward():
+        hid[0, :, pl.ds(0, HID)] = (g / (1.0 + jnp.exp(-g)) * u).astype(BF)
+        scale[0] = jnp.broadcast_to(weights_of(0)[0], (256, HID))
+
+    def hidden_b():
         dh = jnp.zeros((256, HID), F32)
         for k in range(0, D, KSTEP):
             dh = dh + dot_t(rows_of(xb, k), wd[:, pl.ds(k, KSTEP)])
@@ -233,13 +266,27 @@
         kept = dot(pick, saved[...].reshape(256, 2 * HID))
         a, b = kept[:, :HID], kept[:, HID:]
         sigma = 1.0 / (1.0 + jnp.exp(-a))
-        dg = dh * b * (sigma * (1.0 + a * (1.0 - sigma)))
-        du = dh * a * sigma
-        dgu = jnp.concatenate([dg.astype(BF), du.astype(BF)], axis=1)
-        for k in range(NC):
-            for lo in range(k * C, (k + 1) * C, SUB):
-                put(1, lo, dot_t(dgu, wcat[pl.ds(lo, SUB), :]), weight)
-            sib_out(1, k).start()
+        hid[1, :, pl.ds(0, HID)] = (dh * b * (sigma * (1.0 + a * (1.0 - sigma)))).astype(BF)
+        hid[1, :, pl.ds(HID, HID)] = (dh * a * sigma).astype(BF)
+        scale[1] = jnp.broadcast_to(weight, (256, HID))
+
+    def hidden(p):
+        for load in loads[8:11] if p == 0 else loads[11:13]:
+            load.wait()
+        sib_in(p)
+        if p == 0:
+            hidden_f()
+        else:
+            hidden_b()
+
+    def outward(p, k):
+        for lo in range(k * C, (k + 1) * C, SUB):
+            if p == 0:
+                value = dot(hid[0, :, pl.ds(0, HID)], wd[:, pl.ds(lo, SUB)])
+            else:
+                value = dot_t(hid[1], wcat[pl.ds(lo, SUB), :])
+            put(p, lo, value, scale[p][:, :1])
+        sib_out(p, k).start()
 
     lower, upper = pl.ds(0, 2), pl.ds(2, 2)
 
@@ -248,7 +295,7 @@
 
     def far(p, k, d):
         i = 0 if d > 0 else 1
-        return c_copy(p, k, far_s.at[p, k, i], far_r.at[p, k, i], C_FAR_P + i, x_to[d])
+        return c_copy(p, k, far_s.at[p, k, i], far_r.at[p, k, i], C_FAR_P + i, dev(xs[2], y, c) if FAR_DIRECT else x_to[d])
 
     def near(p, k, d, rows, sem):
         i = 0 if d > 0 else 1
@@ -256,6 +303,16 @@
 
     def x_one(p, k):
         sib_out(p, k).wait_recv()
+        if FAR_DIRECT:
+            for i, d in enumerate((1, -1)):
+                near_s[p, k, i] = both(p, k, xs[d], slice(None)).astype(BF)
+                near(p, k, d, lower, C_TWO_P).start()
+                near(p, k, d, upper, C_ONE_P).start()
+            far_s[p, k, 0] = both(p, k, xs[2], lower).astype(BF)
+            far(p, k, 1).start()
+            far_s[p, k, 1] = both(p, k, xs[2], upper).astype(BF)
+            far(p, k, -1).start()
+            return
         far_s[p, k, 0] = both(p, k, xs[2], lower).astype(BF)
         far(p, k, 1).start()
         far_s[p, k, 1] = both(p, k, xs[2], upper).astype(BF)
@@ -266,6 +323,8 @@
         near(p, k, -1, lower, C_ONE_P).start()
 
     def x_two(p, k):
+        if FAR_DIRECT:
+            return
         far(p, k, 1).wait_recv()
         near_s[p, k, 0, lower] = (both(p, k, xs[1], lower) + far_r[p, k, 0].astype(F32)).astype(BF)
         near(p, k, 1, lower, C_TWO_P).start()
@@ -275,10 +334,12 @@
 
     def line(p, k, yi):
         mine = parts[p][k, x, yi, c] + sib_r[p, k, x, yi].astype(F32)
+        if FAR_DIRECT:
+            mine = mine + far_r[p, k, yi // 2, yi % 2].astype(F32)
         return mine + near_r[p, k, 0, yi].astype(F32) + near_r[p, k, 1, yi].astype(F32)
 
     def y_far(p, k):
-        return c_copy(p, k, yfar_s.at[p, k], yfar_r.at[p, k], C_YFAR, y_to[1 if k % 2 == 0 else -1])
+        return c_copy(p, k, yfar_s.at[p, k], yfar_r.at[p, k], C_YFAR, dev(x, ys[2], c, to[p]) if YFAR_DIRECT else y_to[1 if k % 2 == 0 else -1])
 
     def y_near(p, k, d):
         i = 0 if d > 0 else 1
@@ -293,6 +354,18 @@
         near(p, k, -1, lower, C_ONE_P).wait_recv()
         near(p, k, 1, lower, C_TWO_P).wait_recv()
         near(p, k, -1, upper, C_TWO_P).wait_recv()
+        if FAR_DIRECT:
+            far(p, k, 1).wait_recv()
+            far(p, k, -1).wait_recv()
+        if YFAR_DIRECT:
+            for i, d in enumerate((1, -1)):
+                ynear_s[p, k, i] = line(p, k, ys[d]).astype(BF)
+                y_near(p, k, d).start()
+            yfar_s[p, k] = line(p, k, ys[2]).astype(BF)
+            y_far(p, k).start()
+            own_s[p, k] = line(p, k, y).astype(BF)
+            y_own(p, k).start()
+            return
         d = 1 if k % 2 == 0 else -1
         yfar_s[p, k] = line(p, k, ys[2]).astype(BF)
         y_far(p, k).start()
@@ -302,6 +375,8 @@
         y_own(p, k).start()
 
     def y_two(p, k):
+        if YFAR_DIRECT:
+            return
         d = 1 if k % 2 == 0 else -1
         y_far(p, k).wait_recv()
         merged = line(p, k, ys[1] if d > 0 else ys[3]) + yfar_r[p, k].astype(F32)
@@ -309,11 +384,17 @@
         y_near(p, k, d).start()
 
     def finish(p, k):
+        if k == BASE_AT[p]:
+            base_copy(p).wait_recv()
         y_own(p, k).wait_recv()
         y_near(p, k, 1).wait_recv()
         y_near(p, k, -1).wait_recv()
+        if YFAR_DIRECT:
+            y_far(p, k).wait_recv()
         cols = pl.ds(k * C, C)
         total = base_r[p, :, cols].astype(F32) + own_r[p, k].astype(F32)
+        if YFAR_DIRECT:
+            total = total + yfar_r[p, k].astype(F32)
         total = total + ynear_r[p, k, 0].astype(F32) + ynear_r[p, k, 1].astype(F32)
         outs[p][0, :, cols] = total.astype(BF)
 
@@ -327,48 +408,73 @@
         y_far(p, k).wait_send()
         y_own(p, k).wait_send()
 
-    own_out(0)
-    own_out(1)
+    send_x(0, 0)
+    own_y(0)
     x_in(0, 0)
-    y_pass(0)
+    own_y(1)
+    y_in(0, 1)
+    send_x(1, 0)
+    y_in(0, -1)
+    y_in(1, -1)
+    y_last(0)
+    x_in(0, 1)
+    x_in(0, 3)
+    y_in(1, 1)
+    y_last(1)
+    x_in(0, 2)
+    sib_near(0)
+    x_far(0)
+    x_in(1, 0)
+    x_in(1, 3)
+    x_in(1, 1)
+    hidden(0)
+    outward(0, 0)
+    x_in(1, 2)
+    outward(0, 1)
+    outward(0, 2)
+    x_one(0, 0)
+    outward(0, 3)
+    sib_near(1)
+    x_one(0, 2)
+    x_far(1)
+    x_one(0, 1)
+    x_one(0, 3)
+    hidden(1)
+    outward(1, 0)
+    x_two(0, 0)
+    x_two(0, 2)
+    outward(1, 1)
+    x_one(1, 0)
+    outward(1, 2)
+    outward(1, 3)
+    x_two(0, 1)
+    x_two(0, 3)
+    x_one(1, 1)
+    z_ready()
     base_copy(0).start()
     base_copy(1).start()
-    x_in(1, 0)
-    y_pass(1)
-    x_pass(0)
-    x_far(0)
-    x_pass(1)
-    for load in loads[8:11]:
-        load.wait()
-    sib_in(0)
-    forward()
-    x_far(1)
-    for k in range(NC):
-        x_one(0, k)
-    for k in range(NC):
-        x_two(0, k)
-    for load in loads[11:13]:
-        load.wait()
-    sib_in(1)
-    backward()
-    for k in range(NC):
-        y_one(0, k)
-    for k in range(NC):
-        x_one(1, k)
-    for k in range(NC):
-        y_two(0, k)
-    for k in range(NC):
-        x_two(1, k)
-    base_copy(0).wait_recv()
-    for k in range(NC):
-        finish(0, k)
-    for k in range(NC):
-        y_one(1, k)
-    for k in range(NC):
-        y_two(1, k)
-    base_copy(1).wait_recv()
-    for k in range(NC):
-        finish(1, k)
+    y_one(0, 0)
+    x_one(1, 3)
+    y_one(0, 2)
+    x_two(1, 0)
+    y_one(0, 1)
+    x_one(1, 2)
+    y_one(0, 3)
+    x_two(1, 1)
+    x_two(1, 3)
+    y_one(1, 0)
+    x_two(1, 2)
+    finish(0, 0)
+    y_one(1, 1)
+    finish(0, 1)
+    finish(0, 2)
+    y_one(1, 3)
+    finish(0, 3)
+    y_one(1, 2)
+    finish(1, 0)
+    finish(1, 3)
+    finish(1, 1)
+    finish(1, 2)
     for p in range(2):
         gather_sent(p)
         base_copy(p).wait_send()
@@ -408,6 +514,9 @@
             vm((2, NC, ROWS, C), BF),
             vm((2, NC, ROWS, C), BF),
             vm((2, ROWS, D), BF),
+            vm((2, 256, 2 * HID), BF),
+            vm((2, 256, HID), F32),
+            pltpu.SemaphoreType.REGULAR,
             pltpu.SemaphoreType.DMA((2, N_GATHER)),
             pltpu.SemaphoreType.DMA((2, N_GATHER)),
             pltpu.SemaphoreType.DMA((2, NC, N_COMBINE)),
@@ -417,7 +526,7 @@
             pltpu.SemaphoreType.DMA((13,)),
         ],
         compiler_params=pltpu.CompilerParams(
-            collective_id=0, has_side_effects=True, vmem_limit_bytes=48 * 1024 * 1024
+            collective_id=0, has_side_effects=True, vmem_limit_bytes=63 * 1024 * 1024
         ),
         cost_estimate=pl.CostEstimate(flops=1_500_000_000, bytes_accessed=4_000_000, transcendentals=70_000),
     )(*args)

time: 77.7 us -> 61.1 us (0.79)
  the two profiles are of different devices: /device:TPU:8 before, /device:TPU:192 now
where the time goes in v2:
time: 61.1 us; the launch traced here: 60.9 us
  Pallas kernels  58.2 us (95%)
  local copies, waits for them, and re-layouts  2.09 us (3%)
  between operations  0.65 us (1%)
    pallas_call x1, Pallas kernels, local(): pl.pallas_call(kernel, out_shape=(out, out), in_specs=[pl.BlockSpec(memor...  58.2 us
    unnamed x4, local copies, waits for them, and re-layouts  2.09 us

profile of v2, /device:TPU:192, one launch (start us, length us, event | category | flops | bytes accessed | tf_op | source)
XLA Modules:
  0.0 60.9 jit_solution(5015202296618208062)
XLA Ops:
  0.6 58.2 %shard_map.140 = (bf16[1,8,3584]{2,1,0:T(8,128)(2,1)}, bf16[1,8,3584]{2,1,0:T(8,128)(2,1)}) custom-call(bf16[1,8,3584]{2,1,0:T(8,128)(2,1)} %act.1, s32[1,2,8]{2,1,0:T(2,128)} %bitcast.6, s32[1,2,8]{2,1,0:T(2,128)} %bitcast.7, f32[1,2,8]{2,1,0:T(2,128)} %bitcast.8, bf16[1,8,3584]{2,1,0:T(8,128)(2,1)} %grad.1, s32[1,2,8]{2,1,0:T(2,128)} %bitcast.9, ...), custom_call_target="tpu_custom_call" | custom-call | flops 1500000000 | bytes 4000000 | tf_op jit(solution)/shard_map/pallas_call | solution.py:489
  58.8 0.0 copy-start
  58.8 1.5 %copy.17 = bf16[1,8,3584]{2,1,0:T(8,128)(2,1)} copy(bf16[1,8,3584]{2,1,0:T(8,128)(2,1)} %get-tuple-element.4) | data formatting | bytes 114688
  60.3 0.0 copy-done
  60.3 0.6 %copy.18 = bf16[1,8,3584]{2,1,0:T(8,128)(2,1)} copy(bf16[1,8,3584]{2,1,0:T(8,128)(2,1)S(1)} %copy-done) | data formatting | bytes 114688
Async XLA Ops:
  58.8 1.5 %copy-start = (bf16[1,8,3584]{2,1,0:T(8,128)(2,1)S(1)}, bf16[1,8,3584]{2,1,0:T(8,128)(2,1)}, u32[]{:S(2)}) copy-start(bf16[1,8,3584]{2,1,0:T(8,128)(2,1)} %get-tuple-element.5) | copy-start | bytes 172036

commit v3 on v2

--- a/solution.py
+++ b/solution.py
@@ -484,7 +484,7 @@
 
 def local(*args):
     args = [a.transpose(0, 2, 1) if a.shape[-1] == 2 else a for a in args]
-    out = jax.ShapeDtypeStruct((1, ROWS, D), BF)
+    out = pltpu.VMEM((1, ROWS, D), BF)
     vm = pltpu.VMEM
     return pl.pallas_call(
         kernel,

time: 61.1 us -> 59.6 us (0.975)
  local copies, waits for them, and re-layouts: 2.09 us -> 1.25 us
    unnamed x4 -> x2, local copies, waits for them, and re-layouts: 2.09 us -> 1.25 us
    pallas_call x1, Pallas kernels: 58.2 us -> 57.6 us  [local(): pl.pallas_call(kernel, out_shape=(out, out), in_specs=[pl.BlockSpec(memor...]
where the time goes in v3:
time: 59.6 us; the launch traced here: 59.4 us
  Pallas kernels  57.6 us (97%)
  local copies, waits for them, and re-layouts  1.25 us (2%)
  between operations  0.64 us (1%)
    pallas_call x1, Pallas kernels, local(): pl.pallas_call(kernel, out_shape=(out, out), in_specs=[pl.BlockSpec(memor...  57.6 us
    unnamed x2, local copies, waits for them, and re-layouts  1.25 us

profile of v3, /device:TPU:192, one launch (start us, length us, event | category | flops | bytes accessed | tf_op | source)
XLA Modules:
  0.0 59.4 jit_solution(11939730761352643163)
XLA Ops:
  0.6 57.6 %shard_map.140 = (bf16[1,8,3584]{2,1,0:T(8,128)(2,1)S(1)}, bf16[1,8,3584]{2,1,0:T(8,128)(2,1)S(1)}) custom-call(bf16[1,8,3584]{2,1,0:T(8,128)(2,1)} %act.1, s32[1,2,8]{2,1,0:T(2,128)} %bitcast.6, s32[1,2,8]{2,1,0:T(2,128)} %bitcast.7, f32[1,2,8]{2,1,0:T(2,128)} %bitcast.8, bf16[1,8,3584]{2,1,0:T(8,128)(2,1)} %grad.1, s32[1,2,8]{2,1,0:T(2,128)} %bitcast.9, ...), custom_call_target="tpu_custom_call" | custom-call | flops 1500000000 | bytes 4000000 | tf_op jit(solution)/shard_map/pallas_call | solution.py:489
  58.2 0.6 %copy.17 = bf16[1,8,3584]{2,1,0:T(8,128)(2,1)} copy(bf16[1,8,3584]{2,1,0:T(8,128)(2,1)S(1)} %get-tuple-element.2) | data formatting | bytes 114688
  58.8 0.6 %copy.18 = bf16[1,8,3584]{2,1,0:T(8,128)(2,1)} copy(bf16[1,8,3584]{2,1,0:T(8,128)(2,1)S(1)} %get-tuple-element.3) | data formatting | bytes 114688

commit v4 on v3

--- a/solution.py
+++ b/solution.py
@@ -420,61 +420,61 @@
     x_in(0, 1)
     x_in(0, 3)
     y_in(1, 1)
-    y_last(1)
     x_in(0, 2)
     sib_near(0)
+    y_last(1)
+    x_in(1, 0)
     x_far(0)
-    x_in(1, 0)
+    x_in(1, 1)
     x_in(1, 3)
-    x_in(1, 1)
     hidden(0)
     outward(0, 0)
+    outward(0, 1)
     x_in(1, 2)
-    outward(0, 1)
     outward(0, 2)
     x_one(0, 0)
     outward(0, 3)
     sib_near(1)
+    x_one(0, 1)
+    x_far(1)
     x_one(0, 2)
-    x_far(1)
-    x_one(0, 1)
     x_one(0, 3)
     hidden(1)
     outward(1, 0)
     x_two(0, 0)
-    x_two(0, 2)
+    x_two(0, 1)
     outward(1, 1)
     x_one(1, 0)
     outward(1, 2)
-    outward(1, 3)
-    x_two(0, 1)
+    x_two(0, 2)
     x_two(0, 3)
     x_one(1, 1)
+    outward(1, 3)
     z_ready()
     base_copy(0).start()
     base_copy(1).start()
     y_one(0, 0)
+    x_one(1, 2)
+    y_one(0, 1)
+    x_two(1, 0)
     x_one(1, 3)
     y_one(0, 2)
-    x_two(1, 0)
-    y_one(0, 1)
-    x_one(1, 2)
+    x_two(1, 1)
     y_one(0, 3)
-    x_two(1, 1)
+    x_two(1, 2)
+    y_one(1, 0)
     x_two(1, 3)
-    y_one(1, 0)
-    x_two(1, 2)
+    y_one(1, 1)
+    y_one(1, 2)
+    y_one(1, 3)
     finish(0, 0)
-    y_one(1, 1)
     finish(0, 1)
     finish(0, 2)
-    y_one(1, 3)
     finish(0, 3)
-    y_one(1, 2)
     finish(1, 0)
-    finish(1, 3)
     finish(1, 1)
     finish(1, 2)
+    finish(1, 3)
     for p in range(2):
         gather_sent(p)
         base_copy(p).wait_send()

time: 59.6 us -> 58.9 us (0.988)
  Pallas kernels: 57.6 us -> 56.9 us
    pallas_call x1, Pallas kernels: 57.6 us -> 56.9 us  [local(): pl.pallas_call(kernel, out_shape=(out, out), in_specs=[pl.BlockSpec(memor...]
where the time goes in v4:
time: 58.9 us; the launch traced here: 58.8 us
  Pallas kernels  56.9 us (97%)
  local copies, waits for them, and re-layouts  1.25 us (2%)
  between operations  0.64 us (1%)
    pallas_call x1, Pallas kernels, local(): pl.pallas_call(kernel, out_shape=(out, out), in_specs=[pl.BlockSpec(memor...  56.9 us
    unnamed x2, local copies, waits for them, and re-layouts  1.25 us

profile of v4, /device:TPU:192, one launch (start us, length us, event | category | flops | bytes accessed | tf_op | source)
XLA Modules:
  0.0 58.8 jit_solution(13514145983530203955)
XLA Ops:
  0.6 56.9 %shard_map.140 = (bf16[1,8,3584]{2,1,0:T(8,128)(2,1)S(1)}, bf16[1,8,3584]{2,1,0:T(8,128)(2,1)S(1)}) custom-call(bf16[1,8,3584]{2,1,0:T(8,128)(2,1)} %act.1, s32[1,2,8]{2,1,0:T(2,128)} %bitcast.6, s32[1,2,8]{2,1,0:T(2,128)} %bitcast.7, f32[1,2,8]{2,1,0:T(2,128)} %bitcast.8, bf16[1,8,3584]{2,1,0:T(8,128)(2,1)} %grad.1, s32[1,2,8]{2,1,0:T(2,128)} %bitcast.9, ...), custom_call_target="tpu_custom_call" | custom-call | flops 1500000000 | bytes 4000000 | tf_op jit(solution)/shard_map/pallas_call | solution.py:489
  57.5 0.6 %copy.17 = bf16[1,8,3584]{2,1,0:T(8,128)(2,1)} copy(bf16[1,8,3584]{2,1,0:T(8,128)(2,1)S(1)} %get-tuple-element.2) | data formatting | bytes 114688
  58.2 0.6 %copy.18 = bf16[1,8,3584]{2,1,0:T(8,128)(2,1)} copy(bf16[1,8,3584]{2,1,0:T(8,128)(2,1)S(1)} %get-tuple-element.3) | data formatting | bytes 114688
